TPU v7x, 128 devices: a whole 4x4x4 slice. The times are simulated.
128 devices in a mesh: ctx: 16 (over y, x_hi, core), tp: 8 (over x_lo, z).
Axes of the slice: x: 4 (x_hi: 2, x_lo: 2; x = x_hi * 2 + x_lo), y: 4, z: 4, core: 2. Of those that a mesh axis runs over, the one named last changes fastest.
Arguments:
- signal: bfloat16 [8192, 4096], P('ctx', 'tp'), may hold values from -6 to 6
- filter_taps: bfloat16 [8192, 4096], P('ctx', 'tp'), may hold values from -8 to 8
- skip_gain: float32 [4096], P('tp'), may hold values from -4 to 4
- upstream: bfloat16 [8192, 4096], P('ctx', 'tp'), may hold values from -6 to 6
Outputs:
- mixed: bfloat16 [8192, 4096], P('ctx', 'tp')
- signal_grad: bfloat16 [8192, 4096], P('ctx', 'tp')
- filter_grad: bfloat16 [8192, 4096], P('ctx', 'tp')
All inputs are finite; a program needn't handle non-finite values.
Results may differ from a plain program's by a relative error of at most 0.011.
Values may be sent and summed in bfloat16 or wider, within the bound.
No kernel may reach another device: no remote copies, remote signals or barrier semaphores. Data moves between devices by JAX's collectives and lax.ppermute only.
A program may use at most 256 MiB of HBM per device.

v0:
```python
import functools
import math

import jax
import jax.numpy as jnp
import numpy as np
from jax import lax
from jax.experimental import pallas as pl
from jax.experimental.pallas import tpu as pltpu
from jax.sharding import PartitionSpec as P

SEQ_DEV = 512
LANES = 128
CELLS = SEQ_DEV // LANES
QUAD = 4
KINDS = 3
STEP_GROUPS = 4
FILL_BYTES = 58 * 1024 * 1024
ROOM_BYTES = 30 * 1024 * 1024
BF16 = jnp.bfloat16
F32 = jnp.float32


def wide_table(points):
    spot = np.arange(points)
    angle = 2.0 * math.pi * np.outer(spot + 0.25, spot) / points
    return np.kron(np.concatenate([np.cos(angle), -np.sin(angle)]), np.eye(QUAD))


def lane_table():
    spot = np.arange(LANES)
    angle = 2.0 * math.pi * (np.outer(spot, spot) % LANES) / LANES
    cos_part, sin_part = np.cos(angle), np.sin(angle)
    return np.block([[cos_part, -sin_part], [sin_part, cos_part]])


def twist_tables(points):
    angle = 2.0 * math.pi * np.outer(np.arange(points) + 0.25, np.arange(LANES)) / (points * LANES)
    return np.repeat(np.stack([np.cos(angle), np.sin(angle)]), QUAD, axis=1)


def shuffle(shape, row_axis):
    row = lax.broadcasted_iota(jnp.int32, shape, row_axis)
    col = lax.broadcasted_iota(jnp.int32, shape, 1 - row_axis)
    wanted = row // (QUAD * CELLS) * QUAD + row % QUAD + row // QUAD % CELLS * LANES
    return (col == wanted).astype(F32).astype(BF16)


def to_channels(sig_ref, tap_ref, up_ref, out_ref, table, data, sems):
    blocks = data.shape[0]
    per_block = out_ref.shape[0] // blocks

    def fetch(kind, block):
        source = (sig_ref, tap_ref, up_ref)[kind].at[:, pl.ds(block * LANES, LANES)]
        return pltpu.make_async_copy(source, data.at[block, kind], sems.at[block, kind])

    for block in range(blocks):
        for kind in range(KINDS):
            fetch(kind, block).start()
    table[...] = shuffle(table.shape, 0)
    for block in range(blocks):
        for kind in range(KINDS):
            fetch(kind, block).wait()
        wide = [
            jnp.concatenate([data[block, kind, c * LANES : (c + 1) * LANES, :] for c in range(CELLS)], axis=1)
            for kind in range(KINDS)
        ]
        turned = lax.dot_general(
            table[...], jnp.concatenate(wide, axis=0), (((1,), (1,)), ((), ())), preferred_element_type=F32
        ).astype(BF16)
        for kind in range(KINDS):
            piece = turned[:, kind * LANES : (kind + 1) * LANES]
            out_ref[block * per_block : (block + 1) * per_block, kind] = piece.reshape(
                per_block, *out_ref.shape[2:]
            )


def to_positions(in_ref, mix_ref, sig_ref, tap_ref, table, data, sems):
    blocks = data.shape[0]
    per_block = in_ref.shape[0] // blocks

    def flush(kind, block):
        target = (mix_ref, sig_ref, tap_ref)[kind].at[:, pl.ds(block * LANES, LANES)]
        return pltpu.make_async_copy(data.at[block, kind], target, sems.at[block, kind])

    table[...] = shuffle(table.shape, 0)
    for block in range(blocks):
        for kind in range(KINDS):
            piece = in_ref[block * per_block : (block + 1) * per_block, kind].reshape(CELLS * LANES, LANES)
            turned = lax.dot_general(
                piece, table[...], (((0,), (0,)), ((), ())), preferred_element_type=F32
            ).astype(BF16)
            for c in range(CELLS):
                data[block, kind, c * LANES : (c + 1) * LANES, :] = turned[:, c * LANES : (c + 1) * LANES]
            flush(kind, block).start()
    for block in range(blocks):
        for kind in range(KINDS):
            flush(kind, block).wait()


def convolve(x_ref, gain_ref, wide_ref, back_ref, lane_ref, unlane_ref, twist_ref, out_ref, gains):
    slabs, _, groups, cell_rows, _ = x_ref.shape
    rows = slabs * cell_rows
    grad_scale = 1.0 / math.sqrt(slabs * SEQ_DEV)

    shape = (groups * cell_rows, gain_ref.shape[1])
    line = lax.broadcasted_iota(jnp.int32, shape, 0)
    own = lax.axis_index("ctx") * (groups * QUAD) + line // cell_rows * QUAD + line % QUAD
    picked = jnp.where(lax.broadcasted_iota(jnp.int32, shape, 1) == own, gain_ref[...], 0.0)
    gains[...] = jnp.broadcast_to(jnp.sum(picked, axis=1, keepdims=True), gains.shape)

    def step(index, carry):
        units = [(kind, index * STEP_GROUPS + j) for j in range(STEP_GROUPS) for kind in range(KINDS)]
        data = jnp.concatenate([x_ref[:, kind, g].reshape(rows, LANES) for kind, g in units], axis=1)
        wave = jnp.dot(wide_ref[...], data, preferred_element_type=F32)
        spectra = []
        for u in range(len(units)):
            cols = slice(u * LANES, (u + 1) * LANES)
            real, imag = wave[:rows, cols], wave[rows:, cols]
            cos_part, sin_part = twist_ref[0], twist_ref[1]
            band = [real * cos_part + imag * sin_part, imag * cos_part - real * sin_part]
            band = jnp.concatenate([part.astype(BF16) for part in band], axis=1)
            spectra.append(jnp.dot(band, lane_ref[...], preferred_element_type=F32))
        bands = []
        for j in range(STEP_GROUPS):
            (sig_r, sig_i), (tap_r, tap_i), (up_r, up_i) = (
                (part[:, :LANES], part[:, LANES:]) for part in spectra[KINDS * j : KINDS * (j + 1)]
            )
            pairs = (
                (sig_r * tap_r - sig_i * tap_i, sig_r * tap_i + sig_i * tap_r),
                (up_r * tap_r + up_i * tap_i, up_i * tap_r - up_r * tap_i),
                (up_r * sig_r + up_i * sig_i, up_i * sig_r - up_r * sig_i),
            )
            for pair in pairs:
                product = jnp.concatenate([part.astype(BF16) for part in pair], axis=1)
                coef = jnp.dot(product, unlane_ref[...], preferred_element_type=F32)
                real, imag = coef[:, :LANES], coef[:, LANES:]
                cos_part, sin_part = twist_ref[0], twist_ref[1]
                band = [real * cos_part - imag * sin_part, imag * cos_part + real * sin_part]
                bands.append(jnp.concatenate([part.astype(BF16) for part in band], axis=0))
        sums = jnp.dot(back_ref[...], jnp.concatenate(bands, axis=1), preferred_element_type=F32)
        for u, (kind, g) in enumerate(units):
            conv = sums[:, u * LANES : (u + 1) * LANES].reshape(slabs, cell_rows, LANES)
            if kind < 2:
                gain = gains[pl.ds(pl.multiple_of(g * cell_rows, cell_rows), cell_rows), :]
                conv = conv + gain[None] * x_ref[:, 2 * kind, g].astype(F32)
            else:
                conv = conv * grad_scale
            out_ref[:, kind, g] = conv.astype(BF16)
        return carry

    lax.fori_loop(0, groups // STEP_GROUPS, step, 0)


def local(signal, filter_taps, skip_gain, upstream):
    ctx_count = lax.axis_size("ctx")
    chan_count = signal.shape[1]
    groups = chan_count // ctx_count // QUAD
    blocks = chan_count // LANES
    points = ctx_count * CELLS
    pieces = jax.ShapeDtypeStruct((ctx_count, KINDS, groups, CELLS * QUAD, LANES), BF16)
    hbm = pl.BlockSpec(memory_space=pltpu.HBM)
    turning = [
        pltpu.VMEM((CELLS * LANES, CELLS * LANES), BF16),
        pltpu.VMEM((blocks, KINDS, SEQ_DEV, LANES), BF16),
        pltpu.SemaphoreType.DMA((blocks, KINDS)),
    ]
    exchange = functools.partial(lax.all_to_all, axis_name="ctx", split_axis=0, concat_axis=0, tiled=True)

    sent = pl.pallas_call(
        to_channels,
        in_specs=[hbm] * 3,
        out_shape=pieces,
        scratch_shapes=turning,
        compiler_params=pltpu.CompilerParams(vmem_limit_bytes=FILL_BYTES),
        name="to_channels",
    )(signal, filter_taps, upstream)
    whole = exchange(sent)

    wide, lanes = wide_table(points), lane_table()
    results = pl.pallas_call(
        convolve,
        out_shape=pieces,
        scratch_shapes=[pltpu.VMEM((groups * CELLS * QUAD, LANES), F32)],
        compiler_params=pltpu.CompilerParams(vmem_limit_bytes=ROOM_BYTES),
        name="convolve",
    )(
        whole,
        skip_gain.reshape(1, chan_count),
        jnp.asarray(wide, BF16),
        jnp.asarray(wide.T / (points * LANES), BF16),
        jnp.asarray(lanes, BF16),
        jnp.asarray(lanes.T, BF16),
        jnp.asarray(twist_tables(points), F32),
    )
    returned = exchange(results)
    return pl.pallas_call(
        to_positions,
        out_specs=[hbm] * 3,
        out_shape=[jax.ShapeDtypeStruct((SEQ_DEV, chan_count), BF16)] * 3,
        scratch_shapes=turning,
        compiler_params=pltpu.CompilerParams(vmem_limit_bytes=ROOM_BYTES),
        name="to_positions",
    )(returned)


def solution(mesh):
    in_specs = (P("ctx", "tp"), P("ctx", "tp"), P("tp"), P("ctx", "tp"))
    out_specs = (P("ctx", "tp"), P("ctx", "tp"), P("ctx", "tp"))
    return jax.shard_map(local, mesh=mesh, in_specs=in_specs, out_specs=out_specs, check_vma=False)
```

profile of v0, /device:TPU:1, one launch (start us, length us, event | category | flops | bytes accessed | tf_op | source)
XLA Modules:
  0.0 68.7 jit_solution(18430571144521482651)
XLA Ops:
  0.6 4.2 %to_channels.1 = bf16[16,3,8,16,128]{4,3,2,1,0:T(8,128)(2,1)} custom-call(bf16[512,512]{1,0:T(8,128)(2,1)} %sig_ref.1, bf16[512,512]{1,0:T(8,128)(2,1)} %tap_ref.1, bf16[512,512]{1,0:T(8,128)(2,1)} %up_ref.1), custom_call_target="tpu_custom_call" | custom-call | tf_op jit(solution)/shard_map/to_channels/pallas_call | solution.py:170
  4.8 0.0 copy-start
  4.8 0.0 copy-start.1
  4.8 0.0 copy-start.2
  4.8 0.0 copy-start.3
  4.9 0.0 copy-start.4
  4.9 0.0 copy-start.5
  4.9 31.1 %all_to_all.10.x_ref = bf16[16,3,8,16,128]{4,3,2,1,0:T(8,128)(2,1)S(1)} all-to-all(bf16[16,3,8,16,128]{4,3,2,1,0:T(8,128)(2,1)} %to_channels.1), channel_id=1, replica_groups=mesh['ctx'=16,'tp'=8] {'ctx'}, dimensions={0} | all-to-all | bytes 3145728 | tf_op jit(solution)/shard_map/all_to_all | solution.py:178
  36.0 0.0 copy-done
  36.0 0.0 copy-done.1
  36.0 0.0 copy-done.2
  36.0 0.0 copy-done.3
  36.0 0.0 copy-done.4
  36.0 0.0 copy-done.5
  36.0 4.6 %convolve.1 = bf16[16,3,8,16,128]{4,3,2,1,0:T(8,128)(2,1)S(1)} custom-call(bf16[16,3,8,16,128]{4,3,2,1,0:T(8,128)(2,1)S(1)} %all_to_all.10.x_ref, f32[1,512]{1,0:T(1,128)S(1)} %bitcast.1, bf16[512,256]{1,0:T(8,128)(2,1)S(1)} %copy-done.2, bf16[256,512]{1,0:T(8,128)(2,1)S(1)} %copy-done.1, bf16[256,256]{1,0:T(8,128)(2,1)S(1)} %copy-done.4, ...), custom_call_target="tpu_custom_call" | custom-call | tf_op jit(solution)/shard_map/convolve/pallas_call | solution.py:181
  40.6 26.2 %all_to_all.11.in_ref = bf16[16,3,8,16,128]{4,3,2,1,0:T(8,128)(2,1)S(1)} all-to-all(bf16[16,3,8,16,128]{4,3,2,1,0:T(8,128)(2,1)S(1)} %convolve.1), channel_id=1, replica_groups=mesh['ctx'=16,'tp'=8] {'ctx'}, dimensions={0} | all-to-all | bytes 3145728 | tf_op jit(solution)/shard_map/all_to_all | solution.py:196
  66.8 1.9 %to_positions.1 = (bf16[512,512]{1,0:T(8,128)(2,1)}, bf16[512,512]{1,0:T(8,128)(2,1)}, bf16[512,512]{1,0:T(8,128)(2,1)}) custom-call(bf16[16,3,8,16,128]{4,3,2,1,0:T(8,128)(2,1)S(1)} %all_to_all.11.in_ref), custom_call_target="tpu_custom_call" | custom-call | tf_op jit(solution)/shard_map/to_positions/pallas_call | solution.py:197
Async XLA Ops:
  4.8 31.2 %copy-start = (f32[2,256,128]{2,1,0:T(8,128)S(1)}, f32[2,256,128]{2,1,0:T(8,128)}, u32[]{:S(2)}) copy-start(f32[2,256,128]{2,1,0:T(8,128)} %constant.14.clone.twist_ref) | copy-start | bytes 786436
  4.8 31.2 %copy-start.1 = (bf16[256,512]{1,0:T(8,128)(2,1)S(1)}, bf16[256,512]{1,0:T(8,128)(2,1)}, u32[]{:S(2)}) copy-start(bf16[256,512]{1,0:T(8,128)(2,1)} %constant.11.clone.back_ref) | copy-start | bytes 786436
  4.8 31.2 %copy-start.2 = (bf16[512,256]{1,0:T(8,128)(2,1)S(1)}, bf16[512,256]{1,0:T(8,128)(2,1)}, u32[]{:S(2)}) copy-start(bf16[512,256]{1,0:T(8,128)(2,1)} %constant.10.clone.wide_ref) | copy-start | bytes 786436
  4.8 31.2 %copy-start.3 = (bf16[256,256]{1,0:T(8,128)(2,1)S(1)}, bf16[256,256]{1,0:T(8,128)(2,1)}, u32[]{:S(2)}) copy-start(bf16[256,256]{1,0:T(8,128)(2,1)} %constant.13.clone.unlane_ref) | copy-start | bytes 393220
  4.9 31.2 %copy-start.4 = (bf16[256,256]{1,0:T(8,128)(2,1)S(1)}, bf16[256,256]{1,0:T(8,128)(2,1)}, u32[]{:S(2)}) copy-start(bf16[256,256]{1,0:T(8,128)(2,1)} %constant.12.clone.lane_ref) | copy-start | bytes 393220
  4.9 31.2 %copy-start.5 = (f32[512]{0:T(512)S(1)}, f32[512]{0:T(512)}, u32[]{:S(2)}) copy-start(f32[512]{0:T(512)} %param.11) | copy-start | bytes 6148
where the time goes:
time: 69 us; the launch traced here: 68.7 us
  blocking collectives  57.3 us (83%)
  Pallas kernels  10.6 us (15%)
  between operations  0.72 us (1%)
    all_to_all x1, blocking collectives, local(): whole = exchange(sent)  31.1 us
    all_to_all x1, blocking collectives, local(): returned = exchange(results)  26.2 us
    pallas_call x1, Pallas kernels, local(): pl.pallas_call(convolve, out_shape=pieces, scratch_shapes=[pltpu.VMEM((gr...  4.57 us
    pallas_call x1, Pallas kernels, local(): pl.pallas_call(to_channels, in_specs=[hbm] * 3, out_shape=pieces, scratch...  4.17 us
    pallas_call x1, Pallas kernels, local(): pl.pallas_call(to_positions, out_specs=[hbm] * 3, out_shape=[jax.ShapeDty...  1.87 us

commit v1 on v0

--- a/solution.py
+++ b/solution.py
@@ -14,9 +14,9 @@
 CELLS = SEQ_DEV // LANES
 QUAD = 4
 KINDS = 3
-STEP_GROUPS = 4
+STEP_GROUPS = 2
 FILL_BYTES = 58 * 1024 * 1024
-ROOM_BYTES = 30 * 1024 * 1024
+ROOM_BYTES = 32 * 1024 * 1024
 BF16 = jnp.bfloat16
 F32 = jnp.float32
 
@@ -46,7 +46,7 @@
     return (col == wanted).astype(F32).astype(BF16)
 
 
-def to_channels(sig_ref, tap_ref, up_ref, out_ref, table, data, sems):
+def to_channels(sig_ref, tap_ref, up_ref, out_ref, table, data, turned, sems, out_sems):
     blocks = data.shape[0]
     per_block = out_ref.shape[0] // blocks
 
@@ -54,25 +54,34 @@
         source = (sig_ref, tap_ref, up_ref)[kind].at[:, pl.ds(block * LANES, LANES)]
         return pltpu.make_async_copy(source, data.at[block, kind], sems.at[block, kind])
 
+    def flush(block):
+        devices = pl.ds(block * per_block, per_block)
+        return pltpu.make_async_copy(turned.at[devices], out_ref.at[devices], out_sems.at[block])
+
     for block in range(blocks):
         for kind in range(KINDS):
             fetch(kind, block).start()
     table[...] = shuffle(table.shape, 0)
-    for block in range(blocks):
+
+    def turn(block, carry):
         for kind in range(KINDS):
             fetch(kind, block).wait()
         wide = [
             jnp.concatenate([data[block, kind, c * LANES : (c + 1) * LANES, :] for c in range(CELLS)], axis=1)
             for kind in range(KINDS)
         ]
-        turned = lax.dot_general(
+        found = lax.dot_general(
             table[...], jnp.concatenate(wide, axis=0), (((1,), (1,)), ((), ())), preferred_element_type=F32
         ).astype(BF16)
         for kind in range(KINDS):
-            piece = turned[:, kind * LANES : (kind + 1) * LANES]
-            out_ref[block * per_block : (block + 1) * per_block, kind] = piece.reshape(
-                per_block, *out_ref.shape[2:]
-            )
+            piece = found[:, kind * LANES : (kind + 1) * LANES]
+            turned[pl.ds(block * per_block, per_block), kind] = piece.reshape(per_block, *out_ref.shape[2:])
+        flush(block).start()
+        return carry
+
+    lax.fori_loop(0, blocks, turn, 0)
+    for block in range(blocks):
+        flush(block).wait()
 
 
 def to_positions(in_ref, mix_ref, sig_ref, tap_ref, table, data, sems):
@@ -109,8 +118,8 @@
     picked = jnp.where(lax.broadcasted_iota(jnp.int32, shape, 1) == own, gain_ref[...], 0.0)
     gains[...] = jnp.broadcast_to(jnp.sum(picked, axis=1, keepdims=True), gains.shape)
 
-    def step(index, carry):
-        units = [(kind, index * STEP_GROUPS + j) for j in range(STEP_GROUPS) for kind in range(KINDS)]
+    for start in range(0, groups, STEP_GROUPS):
+        units = [(kind, start + j) for j in range(STEP_GROUPS) for kind in range(KINDS)]
         data = jnp.concatenate([x_ref[:, kind, g].reshape(rows, LANES) for kind, g in units], axis=1)
         wave = jnp.dot(wide_ref[...], data, preferred_element_type=F32)
         spectra = []
@@ -142,14 +151,11 @@
         for u, (kind, g) in enumerate(units):
             conv = sums[:, u * LANES : (u + 1) * LANES].reshape(slabs, cell_rows, LANES)
             if kind < 2:
-                gain = gains[pl.ds(pl.multiple_of(g * cell_rows, cell_rows), cell_rows), :]
+                gain = gains[g * cell_rows : (g + 1) * cell_rows, :]
                 conv = conv + gain[None] * x_ref[:, 2 * kind, g].astype(F32)
             else:
                 conv = conv * grad_scale
             out_ref[:, kind, g] = conv.astype(BF16)
-        return carry
-
-    lax.fori_loop(0, groups // STEP_GROUPS, step, 0)
 
 
 def local(signal, filter_taps, skip_gain, upstream):
@@ -170,8 +176,10 @@
     sent = pl.pallas_call(
         to_channels,
         in_specs=[hbm] * 3,
+        out_specs=hbm,
         out_shape=pieces,
-        scratch_shapes=turning,
+        scratch_shapes=turning[:2]
+        + [pltpu.VMEM(pieces.shape, BF16), turning[2], pltpu.SemaphoreType.DMA((blocks,))],
         compiler_params=pltpu.CompilerParams(vmem_limit_bytes=FILL_BYTES),
         name="to_channels",
     )(signal, filter_taps, upstream)

time: 69 us -> 68.1 us (0.987)
  Pallas kernels: 10.6 us -> 9.77 us
where the time goes in v1:
time: 68.1 us; the launch traced here: 67.9 us
  blocking collectives  57.3 us (84%)
  Pallas kernels  9.77 us (14%)
  between operations  0.72 us (1%)
    all_to_all x1, blocking collectives, local(): whole = exchange(sent)  31.1 us
    all_to_all x1, blocking collectives, local(): returned = exchange(results)  26.2 us
    pallas_call x1, Pallas kernels, local(): pl.pallas_call(convolve, out_shape=pieces, scratch_shapes=[pltpu.VMEM((gr...  4.11 us
    pallas_call x1, Pallas kernels, local(): pl.pallas_call(to_channels, in_specs=[hbm] * 3, out_specs=hbm, out_shape=...  3.79 us
    pallas_call x1, Pallas kernels, local(): pl.pallas_call(to_positions, out_specs=[hbm] * 3, out_shape=[jax.ShapeDty...  1.87 us

profile of v1, /device:TPU:1, one launch (start us, length us, event | category | flops | bytes accessed | tf_op | source)
XLA Modules:
  0.0 67.9 jit_solution(1264492867769400065)
XLA Ops:
  0.6 3.8 %to_channels.1 = bf16[16,3,8,16,128]{4,3,2,1,0:T(8,128)(2,1)} custom-call(bf16[512,512]{1,0:T(8,128)(2,1)} %sig_ref.1, bf16[512,512]{1,0:T(8,128)(2,1)} %tap_ref.1, bf16[512,512]{1,0:T(8,128)(2,1)} %up_ref.1), custom_call_target="tpu_custom_call" | custom-call | tf_op jit(solution)/shard_map/to_channels/pallas_call | solution.py:176
  4.4 0.0 copy-start
  4.4 0.0 copy-start.1
  4.5 0.0 copy-start.2
  4.5 0.0 copy-start.3
  4.5 0.0 copy-start.4
  4.5 0.0 copy-start.5
  4.5 31.1 %all_to_all.10.x_ref = bf16[16,3,8,16,128]{4,3,2,1,0:T(8,128)(2,1)S(1)} all-to-all(bf16[16,3,8,16,128]{4,3,2,1,0:T(8,128)(2,1)} %to_channels.1), channel_id=1, replica_groups=mesh['ctx'=16,'tp'=8] {'ctx'}, dimensions={0} | all-to-all | bytes 3145728 | tf_op jit(solution)/shard_map/all_to_all | solution.py:186
  35.6 0.0 copy-done
  35.6 0.0 copy-done.1
  35.6 0.0 copy-done.2
  35.6 0.0 copy-done.3
  35.6 0.0 copy-done.4
  35.6 0.0 copy-done.5
  35.7 4.1 %convolve.1 = bf16[16,3,8,16,128]{4,3,2,1,0:T(8,128)(2,1)S(1)} custom-call(bf16[16,3,8,16,128]{4,3,2,1,0:T(8,128)(2,1)S(1)} %all_to_all.10.x_ref, f32[1,512]{1,0:T(1,128)S(1)} %bitcast.1, bf16[512,256]{1,0:T(8,128)(2,1)S(1)} %copy-done.2, bf16[256,512]{1,0:T(8,128)(2,1)S(1)} %copy-done.1, bf16[256,256]{1,0:T(8,128)(2,1)S(1)} %copy-done.4, ...), custom_call_target="tpu_custom_call" | custom-call | tf_op jit(solution)/shard_map/convolve/pallas_call | solution.py:189
  39.8 26.2 %all_to_all.11.in_ref = bf16[16,3,8,16,128]{4,3,2,1,0:T(8,128)(2,1)S(1)} all-to-all(bf16[16,3,8,16,128]{4,3,2,1,0:T(8,128)(2,1)S(1)} %convolve.1), channel_id=1, replica_groups=mesh['ctx'=16,'tp'=8] {'ctx'}, dimensions={0} | all-to-all | bytes 3145728 | tf_op jit(solution)/shard_map/all_to_all | solution.py:204
  66.0 1.9 %to_positions.1 = (bf16[512,512]{1,0:T(8,128)(2,1)}, bf16[512,512]{1,0:T(8,128)(2,1)}, bf16[512,512]{1,0:T(8,128)(2,1)}) custom-call(bf16[16,3,8,16,128]{4,3,2,1,0:T(8,128)(2,1)S(1)} %all_to_all.11.in_ref), custom_call_target="tpu_custom_call" | custom-call | tf_op jit(solution)/shard_map/to_positions/pallas_call | solution.py:205
Async XLA Ops:
  4.4 31.2 %copy-start = (f32[2,256,128]{2,1,0:T(8,128)S(1)}, f32[2,256,128]{2,1,0:T(8,128)}, u32[]{:S(2)}) copy-start(f32[2,256,128]{2,1,0:T(8,128)} %constant.14.clone.twist_ref) | copy-start | bytes 786436
  4.4 31.2 %copy-start.1 = (bf16[256,512]{1,0:T(8,128)(2,1)S(1)}, bf16[256,512]{1,0:T(8,128)(2,1)}, u32[]{:S(2)}) copy-start(bf16[256,512]{1,0:T(8,128)(2,1)} %constant.11.clone.back_ref) | copy-start | bytes 786436
  4.5 31.2 %copy-start.2 = (bf16[512,256]{1,0:T(8,128)(2,1)S(1)}, bf16[512,256]{1,0:T(8,128)(2,1)}, u32[]{:S(2)}) copy-start(bf16[512,256]{1,0:T(8,128)(2,1)} %constant.10.clone.wide_ref) | copy-start | bytes 786436
  4.5 31.2 %copy-start.3 = (bf16[256,256]{1,0:T(8,128)(2,1)S(1)}, bf16[256,256]{1,0:T(8,128)(2,1)}, u32[]{:S(2)}) copy-start(bf16[256,256]{1,0:T(8,128)(2,1)} %constant.13.clone.unlane_ref) | copy-start | bytes 393220
  4.5 31.2 %copy-start.4 = (bf16[256,256]{1,0:T(8,128)(2,1)S(1)}, bf16[256,256]{1,0:T(8,128)(2,1)}, u32[]{:S(2)}) copy-start(bf16[256,256]{1,0:T(8,128)(2,1)} %constant.12.clone.lane_ref) | copy-start | bytes 393220
  4.5 31.2 %copy-start.5 = (f32[512]{0:T(512)S(1)}, f32[512]{0:T(512)}, u32[]{:S(2)}) copy-start(f32[512]{0:T(512)} %param.11) | copy-start | bytes 6148

commit v2 on v1

--- a/solution.py
+++ b/solution.py
@@ -13,6 +13,8 @@
 LANES = 128
 CELLS = SEQ_DEV // LANES
 QUAD = 4
+PAIR = 2
+SPLITS = CELLS // PAIR
 KINDS = 3
 STEP_GROUPS = 2
 FILL_BYTES = 58 * 1024 * 1024
@@ -42,7 +44,7 @@
 def shuffle(shape, row_axis):
     row = lax.broadcasted_iota(jnp.int32, shape, row_axis)
     col = lax.broadcasted_iota(jnp.int32, shape, 1 - row_axis)
-    wanted = row // (QUAD * CELLS) * QUAD + row % QUAD + row // QUAD % CELLS * LANES
+    wanted = row // (QUAD * PAIR) * QUAD + row % QUAD + row // QUAD % PAIR * LANES
     return (col == wanted).astype(F32).astype(BF16)
 
 
@@ -66,15 +68,22 @@
     def turn(block, carry):
         for kind in range(KINDS):
             fetch(kind, block).wait()
-        wide = [
-            jnp.concatenate([data[block, kind, c * LANES : (c + 1) * LANES, :] for c in range(CELLS)], axis=1)
-            for kind in range(KINDS)
-        ]
-        found = lax.dot_general(
-            table[...], jnp.concatenate(wide, axis=0), (((1,), (1,)), ((), ())), preferred_element_type=F32
-        ).astype(BF16)
-        for kind in range(KINDS):
-            piece = found[:, kind * LANES : (kind + 1) * LANES]
+        halves = []
+        for split in range(SPLITS):
+            wide = [
+                jnp.concatenate(
+                    [data[block, kind, c * LANES : (c + 1) * LANES, :] for c in range(split * PAIR, (split + 1) * PAIR)],
+                    axis=1,
+                )
+                for kind in range(KINDS)
+            ]
+            found = lax.dot_general(
+                table[...], jnp.concatenate(wide, axis=0), (((1,), (1,)), ((), ())), preferred_element_type=F32
+            )
+            halves.append(found.reshape(-1, PAIR * QUAD, KINDS * LANES))
+        found = jnp.concatenate(halves, axis=1).astype(BF16)
+        for kind in range(KINDS):
+            piece = found[:, :, kind * LANES : (kind + 1) * LANES]
             turned[pl.ds(block * per_block, per_block), kind] = piece.reshape(per_block, *out_ref.shape[2:])
         flush(block).start()
         return carry
@@ -95,12 +104,17 @@
     table[...] = shuffle(table.shape, 0)
     for block in range(blocks):
         for kind in range(KINDS):
-            piece = in_ref[block * per_block : (block + 1) * per_block, kind].reshape(CELLS * LANES, LANES)
-            turned = lax.dot_general(
-                piece, table[...], (((0,), (0,)), ((), ())), preferred_element_type=F32
-            ).astype(BF16)
-            for c in range(CELLS):
-                data[block, kind, c * LANES : (c + 1) * LANES, :] = turned[:, c * LANES : (c + 1) * LANES]
+            for split in range(SPLITS):
+                piece = in_ref[block * per_block : (block + 1) * per_block, kind, split]
+                turned = lax.dot_general(
+                    piece.reshape(PAIR * LANES, LANES),
+                    table[...],
+                    (((0,), (0,)), ((), ())),
+                    preferred_element_type=F32,
+                ).astype(BF16)
+                for c in range(PAIR):
+                    start = (split * PAIR + c) * LANES
+                    data[block, kind, start : start + LANES, :] = turned[:, c * LANES : (c + 1) * LANES]
             flush(kind, block).start()
     for block in range(blocks):
         for kind in range(KINDS):
@@ -148,14 +162,21 @@
                 band = [real * cos_part - imag * sin_part, imag * cos_part + real * sin_part]
                 bands.append(jnp.concatenate([part.astype(BF16) for part in band], axis=0))
         sums = jnp.dot(back_ref[...], jnp.concatenate(bands, axis=1), preferred_element_type=F32)
-        for u, (kind, g) in enumerate(units):
-            conv = sums[:, u * LANES : (u + 1) * LANES].reshape(slabs, cell_rows, LANES)
-            if kind < 2:
-                gain = gains[g * cell_rows : (g + 1) * cell_rows, :]
-                conv = conv + gain[None] * x_ref[:, 2 * kind, g].astype(F32)
-            else:
-                conv = conv * grad_scale
-            out_ref[:, kind, g] = conv.astype(BF16)
+        for kind in range(KINDS):
+            convs = []
+            for j in range(STEP_GROUPS):
+                u, g = j * KINDS + kind, start + j
+                conv = sums[:, u * LANES : (u + 1) * LANES].reshape(slabs, cell_rows, LANES)
+                if kind < 2:
+                    gain = gains[g * cell_rows : (g + 1) * cell_rows, :]
+                    conv = conv + gain[None] * x_ref[:, 2 * kind, g].astype(F32)
+                else:
+                    conv = conv * grad_scale
+                convs.append(conv)
+            low, part = start * PAIR * QUAD, PAIR * QUAD
+            for split in range(SPLITS):
+                rows_of = [conv[:, split * part : (split + 1) * part] for conv in convs]
+                out_ref[:, kind, split, low : low + STEP_GROUPS * part] = jnp.concatenate(rows_of, axis=1).astype(BF16)
 
 
 def local(signal, filter_taps, skip_gain, upstream):
@@ -167,7 +188,7 @@
     pieces = jax.ShapeDtypeStruct((ctx_count, KINDS, groups, CELLS * QUAD, LANES), BF16)
     hbm = pl.BlockSpec(memory_space=pltpu.HBM)
     turning = [
-        pltpu.VMEM((CELLS * LANES, CELLS * LANES), BF16),
+        pltpu.VMEM((PAIR * LANES, PAIR * LANES), BF16),
         pltpu.VMEM((blocks, KINDS, SEQ_DEV, LANES), BF16),
         pltpu.SemaphoreType.DMA((blocks, KINDS)),
     ]
@@ -188,7 +209,7 @@
     wide, lanes = wide_table(points), lane_table()
     results = pl.pallas_call(
         convolve,
-        out_shape=pieces,
+        out_shape=jax.ShapeDtypeStruct((ctx_count, KINDS, SPLITS, groups * PAIR * QUAD, LANES), BF16),
         scratch_shapes=[pltpu.VMEM((groups * CELLS * QUAD, LANES), F32)],
         compiler_params=pltpu.CompilerParams(vmem_limit_bytes=ROOM_BYTES),
         name="convolve",

time: 68.1 us -> 67.1 us (0.985)
  Pallas kernels: 9.77 us -> 8.76 us
where the time goes in v2:
time: 67.1 us; the launch traced here: 66.9 us
  blocking collectives  57.3 us (85%)
  Pallas kernels  8.76 us (13%)
  between operations  0.72 us (1%)
    all_to_all x1, blocking collectives, local(): whole = exchange(sent)  31.1 us
    all_to_all x1, blocking collectives, local(): returned = exchange(results)  26.2 us
    pallas_call x1, Pallas kernels, local(): pl.pallas_call(convolve, out_shape=jax.ShapeDtypeStruct((ctx_count, KINDS...  4.1 us
    pallas_call x1, Pallas kernels, local(): pl.pallas_call(to_channels, in_specs=[hbm] * 3, out_specs=hbm, out_shape=...  3.18 us
    pallas_call x1, Pallas kernels, local(): pl.pallas_call(to_positions, out_specs=[hbm] * 3, out_shape=[jax.ShapeDty...  1.48 us

profile of v2, /device:TPU:1, one launch (start us, length us, event | category | flops | bytes accessed | tf_op | source)
XLA Modules:
  0.0 66.9 jit_solution(3425666353533326521)
XLA Ops:
  0.6 3.2 %to_channels.1 = bf16[16,3,8,16,128]{4,3,2,1,0:T(8,128)(2,1)} custom-call(bf16[512,512]{1,0:T(8,128)(2,1)} %sig_ref.1, bf16[512,512]{1,0:T(8,128)(2,1)} %tap_ref.1, bf16[512,512]{1,0:T(8,128)(2,1)} %up_ref.1), custom_call_target="tpu_custom_call" | custom-call | tf_op jit(solution)/shard_map/to_channels/pallas_call | solution.py:197
  3.8 0.0 copy-start
  3.8 0.0 copy-start.1
  3.8 0.0 copy-start.2
  3.9 0.0 copy-start.3
  3.9 0.0 copy-start.4
  3.9 0.0 copy-start.5
  3.9 31.1 %all_to_all.10.x_ref = bf16[16,3,8,16,128]{4,3,2,1,0:T(8,128)(2,1)S(1)} all-to-all(bf16[16,3,8,16,128]{4,3,2,1,0:T(8,128)(2,1)} %to_channels.1), channel_id=1, replica_groups=mesh['ctx'=16,'tp'=8] {'ctx'}, dimensions={0} | all-to-all | bytes 3145728 | tf_op jit(solution)/shard_map/all_to_all | solution.py:207
  35.0 0.0 copy-done
  35.0 0.0 copy-done.1
  35.0 0.0 copy-done.2
  35.0 0.0 copy-done.3
  35.0 0.0 copy-done.4
  35.0 0.0 copy-done.5
  35.1 4.1 %convolve.1 = bf16[16,3,2,64,128]{4,3,2,1,0:T(8,128)(2,1)S(1)} custom-call(bf16[16,3,8,16,128]{4,3,2,1,0:T(8,128)(2,1)S(1)} %all_to_all.10.x_ref, f32[1,512]{1,0:T(1,128)S(1)} %bitcast.1, bf16[512,256]{1,0:T(8,128)(2,1)S(1)} %copy-done.2, bf16[256,512]{1,0:T(8,128)(2,1)S(1)} %copy-done.1, bf16[256,256]{1,0:T(8,128)(2,1)S(1)} %copy-done.4, ...), custom_call_target="tpu_custom_call" | custom-call | tf_op jit(solution)/shard_map/convolve/pallas_call | solution.py:210
  39.2 26.2 %all_to_all.11.in_ref = bf16[16,3,2,64,128]{4,3,2,1,0:T(8,128)(2,1)S(1)} all-to-all(bf16[16,3,2,64,128]{4,3,2,1,0:T(8,128)(2,1)S(1)} %convolve.1), channel_id=1, replica_groups=mesh['ctx'=16,'tp'=8] {'ctx'}, dimensions={0} | all-to-all | bytes 3145728 | tf_op jit(solution)/shard_map/all_to_all | solution.py:225
  65.4 1.5 %to_positions.1 = (bf16[512,512]{1,0:T(8,128)(2,1)}, bf16[512,512]{1,0:T(8,128)(2,1)}, bf16[512,512]{1,0:T(8,128)(2,1)}) custom-call(bf16[16,3,2,64,128]{4,3,2,1,0:T(8,128)(2,1)S(1)} %all_to_all.11.in_ref), custom_call_target="tpu_custom_call" | custom-call | tf_op jit(solution)/shard_map/to_positions/pallas_call | solution.py:226
Async XLA Ops:
  3.8 31.2 %copy-start = (f32[2,256,128]{2,1,0:T(8,128)S(1)}, f32[2,256,128]{2,1,0:T(8,128)}, u32[]{:S(2)}) copy-start(f32[2,256,128]{2,1,0:T(8,128)} %constant.14.clone.twist_ref) | copy-start | bytes 786436
  3.8 31.2 %copy-start.1 = (bf16[256,512]{1,0:T(8,128)(2,1)S(1)}, bf16[256,512]{1,0:T(8,128)(2,1)}, u32[]{:S(2)}) copy-start(bf16[256,512]{1,0:T(8,128)(2,1)} %constant.11.clone.back_ref) | copy-start | bytes 786436
  3.8 31.2 %copy-start.2 = (bf16[512,256]{1,0:T(8,128)(2,1)S(1)}, bf16[512,256]{1,0:T(8,128)(2,1)}, u32[]{:S(2)}) copy-start(bf16[512,256]{1,0:T(8,128)(2,1)} %constant.10.clone.wide_ref) | copy-start | bytes 786436
  3.9 31.2 %copy-start.3 = (bf16[256,256]{1,0:T(8,128)(2,1)S(1)}, bf16[256,256]{1,0:T(8,128)(2,1)}, u32[]{:S(2)}) copy-start(bf16[256,256]{1,0:T(8,128)(2,1)} %constant.13.clone.unlane_ref) | copy-start | bytes 393220
  3.9 31.2 %copy-start.4 = (bf16[256,256]{1,0:T(8,128)(2,1)S(1)}, bf16[256,256]{1,0:T(8,128)(2,1)}, u32[]{:S(2)}) copy-start(bf16[256,256]{1,0:T(8,128)(2,1)} %constant.12.clone.lane_ref) | copy-start | bytes 393220
  3.9 31.2 %copy-start.5 = (f32[512]{0:T(512)S(1)}, f32[512]{0:T(512)}, u32[]{:S(2)}) copy-start(f32[512]{0:T(512)} %param.11) | copy-start | bytes 6148

commit v3 on v2

--- a/solution.py
+++ b/solution.py
@@ -17,7 +17,6 @@
 SPLITS = CELLS // PAIR
 KINDS = 3
 STEP_GROUPS = 2
-FILL_BYTES = 58 * 1024 * 1024
 ROOM_BYTES = 32 * 1024 * 1024
 BF16 = jnp.bfloat16
 F32 = jnp.float32
@@ -48,17 +47,13 @@
     return (col == wanted).astype(F32).astype(BF16)
 
 
-def to_channels(sig_ref, tap_ref, up_ref, out_ref, table, data, turned, sems, out_sems):
+def to_channels(sig_ref, tap_ref, up_ref, out_ref, table, data, sems):
     blocks = data.shape[0]
     per_block = out_ref.shape[0] // blocks
 
     def fetch(kind, block):
         source = (sig_ref, tap_ref, up_ref)[kind].at[:, pl.ds(block * LANES, LANES)]
         return pltpu.make_async_copy(source, data.at[block, kind], sems.at[block, kind])
-
-    def flush(block):
-        devices = pl.ds(block * per_block, per_block)
-        return pltpu.make_async_copy(turned.at[devices], out_ref.at[devices], out_sems.at[block])
 
     for block in range(blocks):
         for kind in range(KINDS):
@@ -84,13 +79,10 @@
         found = jnp.concatenate(halves, axis=1).astype(BF16)
         for kind in range(KINDS):
             piece = found[:, :, kind * LANES : (kind + 1) * LANES]
-            turned[pl.ds(block * per_block, per_block), kind] = piece.reshape(per_block, *out_ref.shape[2:])
-        flush(block).start()
+            out_ref[pl.ds(block * per_block, per_block), kind] = piece.reshape(per_block, *out_ref.shape[2:])
         return carry
 
     lax.fori_loop(0, blocks, turn, 0)
-    for block in range(blocks):
-        flush(block).wait()
 
 
 def to_positions(in_ref, mix_ref, sig_ref, tap_ref, table, data, sems):
@@ -197,13 +189,11 @@
     sent = pl.pallas_call(
         to_channels,
         in_specs=[hbm] * 3,
-        out_specs=hbm,
-        out_shape=pieces,
-        scratch_shapes=turning[:2]
-        + [pltpu.VMEM(pieces.shape, BF16), turning[2], pltpu.SemaphoreType.DMA((blocks,))],
-        compiler_params=pltpu.CompilerParams(vmem_limit_bytes=FILL_BYTES),
+        out_shape=pltpu.VMEM(pieces.shape, BF16),
+        scratch_shapes=turning,
+        compiler_params=pltpu.CompilerParams(vmem_limit_bytes=ROOM_BYTES),
         name="to_channels",
-    )(signal, filter_taps, upstream)
+    )(*(pltpu.with_memory_space_constraint(x, pltpu.HBM) for x in (signal, filter_taps, upstream)))
     whole = exchange(sent)
 
     wide, lanes = wide_table(points), lane_table()

time: 67.1 us -> 66.5 us (level)
    pallas_call x1, Pallas kernels: 3.18 us -> 2.39 us  [local(): pl.pallas_call(to_channels, in_specs=[hbm] * 3, out_shape=pltpu.VMEM(piec...]
where the time goes in v3:
time: 66.5 us; the launch traced here: 66.3 us
  blocking collectives  57.1 us (86%)
  Pallas kernels  8.36 us (13%)
  between operations  0.72 us (1%)
    all_to_all x1, blocking collectives, local(): whole = exchange(sent)  30.9 us
    all_to_all x1, blocking collectives, local(): returned = exchange(results)  26.2 us
    pallas_call x1, Pallas kernels, local(): pl.pallas_call(convolve, out_shape=jax.ShapeDtypeStruct((ctx_count, KINDS...  4.5 us
    pallas_call x1, Pallas kernels, local(): pl.pallas_call(to_channels, in_specs=[hbm] * 3, out_shape=pltpu.VMEM(piec...  2.39 us
    pallas_call x1, Pallas kernels, local(): pl.pallas_call(to_positions, out_specs=[hbm] * 3, out_shape=[jax.ShapeDty...  1.48 us

profile of v3, /device:TPU:1, one launch (start us, length us, event | category | flops | bytes accessed | tf_op | source)
XLA Modules:
  0.0 66.3 jit_solution(17906639553706641523)
XLA Ops:
  0.6 2.4 %to_channels.1 = bf16[16,3,8,16,128]{4,3,2,1,0:T(8,128)(2,1)S(1)} custom-call(bf16[512,512]{1,0:T(8,128)(2,1)} %sig_ref.1, bf16[512,512]{1,0:T(8,128)(2,1)} %tap_ref.1, bf16[512,512]{1,0:T(8,128)(2,1)} %up_ref.1), custom_call_target="tpu_custom_call" | custom-call | tf_op jit(solution)/shard_map/to_channels/pallas_call | solution.py:189
  3.0 0.0 copy-start
  3.0 0.0 copy-start.1
  3.1 0.0 copy-start.2
  3.1 0.0 copy-start.3
  3.1 0.0 copy-start.4
  3.1 0.0 copy-start.5
  3.1 30.9 %all_to_all.10.x_ref = bf16[16,3,8,16,128]{4,3,2,1,0:T(8,128)(2,1)S(1)} all-to-all(bf16[16,3,8,16,128]{4,3,2,1,0:T(8,128)(2,1)S(1)} %to_channels.1), channel_id=1, replica_groups=mesh['ctx'=16,'tp'=8] {'ctx'}, dimensions={0} | all-to-all | bytes 3145728 | tf_op jit(solution)/shard_map/all_to_all | solution.py:197
  34.0 0.0 copy-done
  34.0 0.0 copy-done.1
  34.0 0.0 copy-done.2
  34.0 0.0 copy-done.3
  34.0 0.0 copy-done.4
  34.0 0.0 copy-done.5
  34.0 4.5 %convolve.1 = bf16[16,3,2,64,128]{4,3,2,1,0:T(8,128)(2,1)S(1)} custom-call(bf16[16,3,8,16,128]{4,3,2,1,0:T(8,128)(2,1)S(1)} %all_to_all.10.x_ref, f32[1,512]{1,0:T(1,128)S(1)} %bitcast.1, bf16[512,256]{1,0:T(8,128)(2,1)S(1)} %copy-done.2, bf16[256,512]{1,0:T(8,128)(2,1)S(1)} %copy-done.1, bf16[256,256]{1,0:T(8,128)(2,1)S(1)} %copy-done.4, ...), custom_call_target="tpu_custom_call" | custom-call | tf_op jit(solution)/shard_map/convolve/pallas_call | solution.py:200
  38.6 26.2 %all_to_all.11.in_ref = bf16[16,3,2,64,128]{4,3,2,1,0:T(8,128)(2,1)S(1)} all-to-all(bf16[16,3,2,64,128]{4,3,2,1,0:T(8,128)(2,1)S(1)} %convolve.1), channel_id=1, replica_groups=mesh['ctx'=16,'tp'=8] {'ctx'}, dimensions={0} | all-to-all | bytes 3145728 | tf_op jit(solution)/shard_map/all_to_all | solution.py:215
  64.8 1.5 %to_positions.1 = (bf16[512,512]{1,0:T(8,128)(2,1)}, bf16[512,512]{1,0:T(8,128)(2,1)}, bf16[512,512]{1,0:T(8,128)(2,1)}) custom-call(bf16[16,3,2,64,128]{4,3,2,1,0:T(8,128)(2,1)S(1)} %all_to_all.11.in_ref), custom_call_target="tpu_custom_call" | custom-call | tf_op jit(solution)/shard_map/to_positions/pallas_call | solution.py:216
Async XLA Ops:
  3.0 31.0 %copy-start = (f32[2,256,128]{2,1,0:T(8,128)S(1)}, f32[2,256,128]{2,1,0:T(8,128)}, u32[]{:S(2)}) copy-start(f32[2,256,128]{2,1,0:T(8,128)} %constant.14.clone.twist_ref) | copy-start | bytes 786436
  3.0 31.0 %copy-start.1 = (bf16[256,512]{1,0:T(8,128)(2,1)S(1)}, bf16[256,512]{1,0:T(8,128)(2,1)}, u32[]{:S(2)}) copy-start(bf16[256,512]{1,0:T(8,128)(2,1)} %constant.11.clone.back_ref) | copy-start | bytes 786436
  3.1 31.0 %copy-start.2 = (bf16[512,256]{1,0:T(8,128)(2,1)S(1)}, bf16[512,256]{1,0:T(8,128)(2,1)}, u32[]{:S(2)}) copy-start(bf16[512,256]{1,0:T(8,128)(2,1)} %constant.10.clone.wide_ref) | copy-start | bytes 786436
  3.1 31.0 %copy-start.3 = (bf16[256,256]{1,0:T(8,128)(2,1)S(1)}, bf16[256,256]{1,0:T(8,128)(2,1)}, u32[]{:S(2)}) copy-start(bf16[256,256]{1,0:T(8,128)(2,1)} %constant.13.clone.unlane_ref) | copy-start | bytes 393220
  3.1 31.0 %copy-start.4 = (bf16[256,256]{1,0:T(8,128)(2,1)S(1)}, bf16[256,256]{1,0:T(8,128)(2,1)}, u32[]{:S(2)}) copy-start(bf16[256,256]{1,0:T(8,128)(2,1)} %constant.12.clone.lane_ref) | copy-start | bytes 393220
  3.1 30.9 %copy-start.5 = (f32[512]{0:T(512)S(1)}, f32[512]{0:T(512)}, u32[]{:S(2)}) copy-start(f32[512]{0:T(512)} %param.11) | copy-start | bytes 6148

commit v4 on v3

--- a/solution.py
+++ b/solution.py
@@ -17,6 +17,8 @@
 SPLITS = CELLS // PAIR
 KINDS = 3
 STEP_GROUPS = 2
+WIDE_SCALE = 1.9925
+LANE_SCALE = 1.625
 ROOM_BYTES = 32 * 1024 * 1024
 BF16 = jnp.bfloat16
 F32 = jnp.float32
@@ -51,18 +53,19 @@
     blocks = data.shape[0]
     per_block = out_ref.shape[0] // blocks
 
-    def fetch(kind, block):
-        source = (sig_ref, tap_ref, up_ref)[kind].at[:, pl.ds(block * LANES, LANES)]
-        return pltpu.make_async_copy(source, data.at[block, kind], sems.at[block, kind])
+    def fetch(kind, block, low, size):
+        source = (sig_ref, tap_ref, up_ref)[kind].at[pl.ds(low, size), pl.ds(block * LANES, LANES)]
+        return pltpu.make_async_copy(source, data.at[block, kind, pl.ds(low, size), :], sems.at[block, kind])
 
     for block in range(blocks):
-        for kind in range(KINDS):
-            fetch(kind, block).start()
+        for low in range(0, SEQ_DEV, LANES):
+            for kind in range(KINDS):
+                fetch(kind, block, low, LANES).start()
     table[...] = shuffle(table.shape, 0)
 
     def turn(block, carry):
         for kind in range(KINDS):
-            fetch(kind, block).wait()
+            fetch(kind, block, 0, SEQ_DEV).wait()
         halves = []
         for split in range(SPLITS):
             wide = [
@@ -196,7 +199,7 @@
     )(*(pltpu.with_memory_space_constraint(x, pltpu.HBM) for x in (signal, filter_taps, upstream)))
     whole = exchange(sent)
 
-    wide, lanes = wide_table(points), lane_table()
+    wide, lanes = WIDE_SCALE * wide_table(points), LANE_SCALE * lane_table()
     results = pl.pallas_call(
         convolve,
         out_shape=jax.ShapeDtypeStruct((ctx_count, KINDS, SPLITS, groups * PAIR * QUAD, LANES), BF16),
@@ -210,7 +213,7 @@
         jnp.asarray(wide.T / (points * LANES), BF16),
         jnp.asarray(lanes, BF16),
         jnp.asarray(lanes.T, BF16),
-        jnp.asarray(twist_tables(points), F32),
+        jnp.asarray(twist_tables(points) / (WIDE_SCALE * LANE_SCALE), F32),
     )
     returned = exchange(results)
     return pl.pallas_call(

time: 66.5 us -> 66.4 us (level)
  no operation moved by 1% of the time
where the time goes in v4:
time: 66.4 us; the launch traced here: 66.2 us
  blocking collectives  57.1 us (86%)
  Pallas kernels  8.26 us (12%)
  between operations  0.72 us (1%)
    all_to_all x1, blocking collectives, local(): whole = exchange(sent)  30.9 us
    all_to_all x1, blocking collectives, local(): returned = exchange(results)  26.2 us
    pallas_call x1, Pallas kernels, local(): pl.pallas_call(convolve, out_shape=jax.ShapeDtypeStruct((ctx_count, KINDS...  4.5 us
    pallas_call x1, Pallas kernels, local(): pl.pallas_call(to_channels, in_specs=[hbm] * 3, out_shape=pltpu.VMEM(piec...  2.29 us
    pallas_call x1, Pallas kernels, local(): pl.pallas_call(to_positions, out_specs=[hbm] * 3, out_shape=[jax.ShapeDty...  1.48 us

profile of v4, /device:TPU:1, one launch (start us, length us, event | category | flops | bytes accessed | tf_op | source)
XLA Modules:
  0.0 66.2 jit_solution(6903352060671339794)
XLA Ops:
  0.6 2.3 %to_channels.1 = bf16[16,3,8,16,128]{4,3,2,1,0:T(8,128)(2,1)S(1)} custom-call(bf16[512,512]{1,0:T(8,128)(2,1)} %sig_ref.1, bf16[512,512]{1,0:T(8,128)(2,1)} %tap_ref.1, bf16[512,512]{1,0:T(8,128)(2,1)} %up_ref.1), custom_call_target="tpu_custom_call" | custom-call | tf_op jit(solution)/shard_map/to_channels/pallas_call | solution.py:192
  2.9 0.0 copy-start
  2.9 0.0 copy-start.1
  3.0 0.0 copy-start.2
  3.0 0.0 copy-start.3
  3.0 0.0 copy-start.4
  3.0 0.0 copy-start.5
  3.0 30.9 %all_to_all.10.x_ref = bf16[16,3,8,16,128]{4,3,2,1,0:T(8,128)(2,1)S(1)} all-to-all(bf16[16,3,8,16,128]{4,3,2,1,0:T(8,128)(2,1)S(1)} %to_channels.1), channel_id=1, replica_groups=mesh['ctx'=16,'tp'=8] {'ctx'}, dimensions={0} | all-to-all | bytes 3145728 | tf_op jit(solution)/shard_map/all_to_all | solution.py:200
  33.9 0.0 copy-done
  33.9 0.0 copy-done.1
  33.9 0.0 copy-done.2
  33.9 0.0 copy-done.3
  33.9 0.0 copy-done.4
  33.9 0.0 copy-done.5
  33.9 4.5 %convolve.1 = bf16[16,3,2,64,128]{4,3,2,1,0:T(8,128)(2,1)S(1)} custom-call(bf16[16,3,8,16,128]{4,3,2,1,0:T(8,128)(2,1)S(1)} %all_to_all.10.x_ref, f32[1,512]{1,0:T(1,128)S(1)} %bitcast.1, bf16[512,256]{1,0:T(8,128)(2,1)S(1)} %copy-done.2, bf16[256,512]{1,0:T(8,128)(2,1)S(1)} %copy-done.1, bf16[256,256]{1,0:T(8,128)(2,1)S(1)} %copy-done.4, ...), custom_call_target="tpu_custom_call" | custom-call | tf_op jit(solution)/shard_map/convolve/pallas_call | solution.py:203
  38.5 26.2 %all_to_all.11.in_ref = bf16[16,3,2,64,128]{4,3,2,1,0:T(8,128)(2,1)S(1)} all-to-all(bf16[16,3,2,64,128]{4,3,2,1,0:T(8,128)(2,1)S(1)} %convolve.1), channel_id=1, replica_groups=mesh['ctx'=16,'tp'=8] {'ctx'}, dimensions={0} | all-to-all | bytes 3145728 | tf_op jit(solution)/shard_map/all_to_all | solution.py:218
  64.7 1.5 %to_positions.1 = (bf16[512,512]{1,0:T(8,128)(2,1)}, bf16[512,512]{1,0:T(8,128)(2,1)}, bf16[512,512]{1,0:T(8,128)(2,1)}) custom-call(bf16[16,3,2,64,128]{4,3,2,1,0:T(8,128)(2,1)S(1)} %all_to_all.11.in_ref), custom_call_target="tpu_custom_call" | custom-call | tf_op jit(solution)/shard_map/to_positions/pallas_call | solution.py:219
Async XLA Ops:
  2.9 31.0 %copy-start = (f32[2,256,128]{2,1,0:T(8,128)S(1)}, f32[2,256,128]{2,1,0:T(8,128)}, u32[]{:S(2)}) copy-start(f32[2,256,128]{2,1,0:T(8,128)} %constant.14.clone.twist_ref) | copy-start | bytes 786436
  2.9 31.0 %copy-start.1 = (bf16[256,512]{1,0:T(8,128)(2,1)S(1)}, bf16[256,512]{1,0:T(8,128)(2,1)}, u32[]{:S(2)}) copy-start(bf16[256,512]{1,0:T(8,128)(2,1)} %constant.11.clone.back_ref) | copy-start | bytes 786436
  3.0 31.0 %copy-start.2 = (bf16[512,256]{1,0:T(8,128)(2,1)S(1)}, bf16[512,256]{1,0:T(8,128)(2,1)}, u32[]{:S(2)}) copy-start(bf16[512,256]{1,0:T(8,128)(2,1)} %constant.10.clone.wide_ref) | copy-start | bytes 786436
  3.0 31.0 %copy-start.3 = (bf16[256,256]{1,0:T(8,128)(2,1)S(1)}, bf16[256,256]{1,0:T(8,128)(2,1)}, u32[]{:S(2)}) copy-start(bf16[256,256]{1,0:T(8,128)(2,1)} %constant.13.clone.unlane_ref) | copy-start | bytes 393220
  3.0 31.0 %copy-start.4 = (bf16[256,256]{1,0:T(8,128)(2,1)S(1)}, bf16[256,256]{1,0:T(8,128)(2,1)}, u32[]{:S(2)}) copy-start(bf16[256,256]{1,0:T(8,128)(2,1)} %constant.12.clone.lane_ref) | copy-start | bytes 393220
  3.0 30.9 %copy-start.5 = (f32[512]{0:T(512)S(1)}, f32[512]{0:T(512)}, u32[]{:S(2)}) copy-start(f32[512]{0:T(512)} %param.11) | copy-start | bytes 6148

commit v5 on v4

--- a/solution.py
+++ b/solution.py
@@ -17,8 +17,6 @@
 SPLITS = CELLS // PAIR
 KINDS = 3
 STEP_GROUPS = 2
-WIDE_SCALE = 1.9925
-LANE_SCALE = 1.625
 ROOM_BYTES = 32 * 1024 * 1024
 BF16 = jnp.bfloat16
 F32 = jnp.float32
@@ -92,9 +90,9 @@
     blocks = data.shape[0]
     per_block = in_ref.shape[0] // blocks
 
-    def flush(kind, block):
-        target = (mix_ref, sig_ref, tap_ref)[kind].at[:, pl.ds(block * LANES, LANES)]
-        return pltpu.make_async_copy(data.at[block, kind], target, sems.at[block, kind])
+    def flush(kind, block, low, size):
+        target = (mix_ref, sig_ref, tap_ref)[kind].at[pl.ds(low, size), pl.ds(block * LANES, LANES)]
+        return pltpu.make_async_copy(data.at[block, kind, pl.ds(low, size), :], target, sems.at[block, kind])
 
     table[...] = shuffle(table.shape, 0)
     for block in range(blocks):
@@ -110,10 +108,10 @@
                 for c in range(PAIR):
                     start = (split * PAIR + c) * LANES
                     data[block, kind, start : start + LANES, :] = turned[:, c * LANES : (c + 1) * LANES]
-            flush(kind, block).start()
+                flush(kind, block, split * PAIR * LANES, PAIR * LANES).start()
     for block in range(blocks):
         for kind in range(KINDS):
-            flush(kind, block).wait()
+            flush(kind, block, 0, SEQ_DEV).wait()
 
 
 def convolve(x_ref, gain_ref, wide_ref, back_ref, lane_ref, unlane_ref, twist_ref, out_ref, gains):
@@ -199,7 +197,7 @@
     )(*(pltpu.with_memory_space_constraint(x, pltpu.HBM) for x in (signal, filter_taps, upstream)))
     whole = exchange(sent)
 
-    wide, lanes = WIDE_SCALE * wide_table(points), LANE_SCALE * lane_table()
+    wide, lanes = wide_table(points), lane_table()
     results = pl.pallas_call(
         convolve,
         out_shape=jax.ShapeDtypeStruct((ctx_count, KINDS, SPLITS, groups * PAIR * QUAD, LANES), BF16),
@@ -213,7 +211,7 @@
         jnp.asarray(wide.T / (points * LANES), BF16),
         jnp.asarray(lanes, BF16),
         jnp.asarray(lanes.T, BF16),
-        jnp.asarray(twist_tables(points) / (WIDE_SCALE * LANE_SCALE), F32),
+        jnp.asarray(twist_tables(points), F32),
     )
     returned = exchange(results)
     return pl.pallas_call(

time: 66.4 us -> 66.4 us (level)
  no operation moved by 1% of the time
where the time goes in v5:
time: 66.4 us; the launch traced here: 66.1 us
  blocking collectives  57.1 us (86%)
  Pallas kernels  8.23 us (12%)
  between operations  0.72 us (1%)
    all_to_all x1, blocking collectives, local(): whole = exchange(sent)  30.9 us
    all_to_all x1, blocking collectives, local(): returned = exchange(results)  26.2 us
    pallas_call x1, Pallas kernels, local(): pl.pallas_call(convolve, out_shape=jax.ShapeDtypeStruct((ctx_count, KINDS...  4.5 us
    pallas_call x1, Pallas kernels, local(): pl.pallas_call(to_channels, in_specs=[hbm] * 3, out_shape=pltpu.VMEM(piec...  2.29 us
    pallas_call x1, Pallas kernels, local(): pl.pallas_call(to_positions, out_specs=[hbm] * 3, out_shape=[jax.ShapeDty...  1.44 us

profile of v5, /device:TPU:1, one launch (start us, length us, event | category | flops | bytes accessed | tf_op | source)
XLA Modules:
  0.0 66.1 jit_solution(1499338814722851168)
XLA Ops:
  0.6 2.3 %to_channels.1 = bf16[16,3,8,16,128]{4,3,2,1,0:T(8,128)(2,1)S(1)} custom-call(bf16[512,512]{1,0:T(8,128)(2,1)} %sig_ref.1, bf16[512,512]{1,0:T(8,128)(2,1)} %tap_ref.1, bf16[512,512]{1,0:T(8,128)(2,1)} %up_ref.1), custom_call_target="tpu_custom_call" | custom-call | tf_op jit(solution)/shard_map/to_channels/pallas_call | solution.py:190
  2.9 0.0 copy-start
  2.9 0.0 copy-start.1
  3.0 0.0 copy-start.2
  3.0 0.0 copy-start.3
  3.0 0.0 copy-start.4
  3.0 0.0 copy-start.5
  3.0 30.9 %all_to_all.10.x_ref = bf16[16,3,8,16,128]{4,3,2,1,0:T(8,128)(2,1)S(1)} all-to-all(bf16[16,3,8,16,128]{4,3,2,1,0:T(8,128)(2,1)S(1)} %to_channels.1), channel_id=1, replica_groups=mesh['ctx'=16,'tp'=8] {'ctx'}, dimensions={0} | all-to-all | bytes 3145728 | tf_op jit(solution)/shard_map/all_to_all | solution.py:198
  33.9 0.0 copy-done
  33.9 0.0 copy-done.1
  33.9 0.0 copy-done.2
  33.9 0.0 copy-done.3
  33.9 0.0 copy-done.4
  33.9 0.0 copy-done.5
  33.9 4.5 %convolve.1 = bf16[16,3,2,64,128]{4,3,2,1,0:T(8,128)(2,1)S(1)} custom-call(bf16[16,3,8,16,128]{4,3,2,1,0:T(8,128)(2,1)S(1)} %all_to_all.10.x_ref, f32[1,512]{1,0:T(1,128)S(1)} %bitcast.1, bf16[512,256]{1,0:T(8,128)(2,1)S(1)} %copy-done.2, bf16[256,512]{1,0:T(8,128)(2,1)S(1)} %copy-done.1, bf16[256,256]{1,0:T(8,128)(2,1)S(1)} %copy-done.4, ...), custom_call_target="tpu_custom_call" | custom-call | tf_op jit(solution)/shard_map/convolve/pallas_call | solution.py:201
  38.5 26.2 %all_to_all.11.in_ref = bf16[16,3,2,64,128]{4,3,2,1,0:T(8,128)(2,1)S(1)} all-to-all(bf16[16,3,2,64,128]{4,3,2,1,0:T(8,128)(2,1)S(1)} %convolve.1), channel_id=1, replica_groups=mesh['ctx'=16,'tp'=8] {'ctx'}, dimensions={0} | all-to-all | bytes 3145728 | tf_op jit(solution)/shard_map/all_to_all | solution.py:216
  64.7 1.4 %to_positions.1 = (bf16[512,512]{1,0:T(8,128)(2,1)}, bf16[512,512]{1,0:T(8,128)(2,1)}, bf16[512,512]{1,0:T(8,128)(2,1)}) custom-call(bf16[16,3,2,64,128]{4,3,2,1,0:T(8,128)(2,1)S(1)} %all_to_all.11.in_ref), custom_call_target="tpu_custom_call" | custom-call | tf_op jit(solution)/shard_map/to_positions/pallas_call | solution.py:217
Async XLA Ops:
  2.9 31.0 %copy-start = (f32[2,256,128]{2,1,0:T(8,128)S(1)}, f32[2,256,128]{2,1,0:T(8,128)}, u32[]{:S(2)}) copy-start(f32[2,256,128]{2,1,0:T(8,128)} %constant.14.clone.twist_ref) | copy-start | bytes 786436
  2.9 31.0 %copy-start.1 = (bf16[256,512]{1,0:T(8,128)(2,1)S(1)}, bf16[256,512]{1,0:T(8,128)(2,1)}, u32[]{:S(2)}) copy-start(bf16[256,512]{1,0:T(8,128)(2,1)} %constant.11.clone.back_ref) | copy-start | bytes 786436
  3.0 31.0 %copy-start.2 = (bf16[512,256]{1,0:T(8,128)(2,1)S(1)}, bf16[512,256]{1,0:T(8,128)(2,1)}, u32[]{:S(2)}) copy-start(bf16[512,256]{1,0:T(8,128)(2,1)} %constant.10.clone.wide_ref) | copy-start | bytes 786436
  3.0 31.0 %copy-start.3 = (bf16[256,256]{1,0:T(8,128)(2,1)S(1)}, bf16[256,256]{1,0:T(8,128)(2,1)}, u32[]{:S(2)}) copy-start(bf16[256,256]{1,0:T(8,128)(2,1)} %constant.13.clone.unlane_ref) | copy-start | bytes 393220
  3.0 31.0 %copy-start.4 = (bf16[256,256]{1,0:T(8,128)(2,1)S(1)}, bf16[256,256]{1,0:T(8,128)(2,1)}, u32[]{:S(2)}) copy-start(bf16[256,256]{1,0:T(8,128)(2,1)} %constant.12.clone.lane_ref) | copy-start | bytes 393220
  3.0 30.9 %copy-start.5 = (f32[512]{0:T(512)S(1)}, f32[512]{0:T(512)}, u32[]{:S(2)}) copy-start(f32[512]{0:T(512)} %param.11) | copy-start | bytes 6148

commit v6 on v3

--- a/solution.py
+++ b/solution.py
@@ -126,16 +126,17 @@
 
     for start in range(0, groups, STEP_GROUPS):
         units = [(kind, start + j) for j in range(STEP_GROUPS) for kind in range(KINDS)]
+        order = [j * KINDS + kind for kind in range(KINDS) for j in range(STEP_GROUPS)]
         data = jnp.concatenate([x_ref[:, kind, g].reshape(rows, LANES) for kind, g in units], axis=1)
         wave = jnp.dot(wide_ref[...], data, preferred_element_type=F32)
-        spectra = []
-        for u in range(len(units)):
+        spectra = [None] * len(units)
+        for u in order:
             cols = slice(u * LANES, (u + 1) * LANES)
             real, imag = wave[:rows, cols], wave[rows:, cols]
             cos_part, sin_part = twist_ref[0], twist_ref[1]
             band = [real * cos_part + imag * sin_part, imag * cos_part - real * sin_part]
             band = jnp.concatenate([part.astype(BF16) for part in band], axis=1)
-            spectra.append(jnp.dot(band, lane_ref[...], preferred_element_type=F32))
+            spectra[u] = jnp.dot(band, lane_ref[...], preferred_element_type=F32)
         bands = []
         for j in range(STEP_GROUPS):
             (sig_r, sig_i), (tap_r, tap_i), (up_r, up_i) = (

time: 66.5 us -> 66.5 us (level)
  no operation moved by 1% of the time
where the time goes in v6:
time: 66.5 us; the launch traced here: 66.3 us
  blocking collectives  57.1 us (86%)
  Pallas kernels  8.42 us (13%)
  between operations  0.72 us (1%)
    all_to_all x1, blocking collectives, local(): whole = exchange(sent)  30.9 us
    all_to_all x1, blocking collectives, local(): returned = exchange(results)  26.2 us
    pallas_call x1, Pallas kernels, local(): pl.pallas_call(convolve, out_shape=jax.ShapeDtypeStruct((ctx_count, KINDS...  4.55 us
    pallas_call x1, Pallas kernels, local(): pl.pallas_call(to_channels, in_specs=[hbm] * 3, out_shape=pltpu.VMEM(piec...  2.39 us
    pallas_call x1, Pallas kernels, local(): pl.pallas_call(to_positions, out_specs=[hbm] * 3, out_shape=[jax.ShapeDty...  1.48 us

profile of v6, /device:TPU:1, one launch (start us, length us, event | category | flops | bytes accessed | tf_op | source)
XLA Modules:
  0.0 66.3 jit_solution(18313797021572839556)
XLA Ops:
  0.6 2.4 %to_channels.1 = bf16[16,3,8,16,128]{4,3,2,1,0:T(8,128)(2,1)S(1)} custom-call(bf16[512,512]{1,0:T(8,128)(2,1)} %sig_ref.1, bf16[512,512]{1,0:T(8,128)(2,1)} %tap_ref.1, bf16[512,512]{1,0:T(8,128)(2,1)} %up_ref.1), custom_call_target="tpu_custom_call" | custom-call | tf_op jit(solution)/shard_map/to_channels/pallas_call | solution.py:190
  3.0 0.0 copy-start
  3.0 0.0 copy-start.1
  3.1 0.0 copy-start.2
  3.1 0.0 copy-start.3
  3.1 0.0 copy-start.4
  3.1 0.0 copy-start.5
  3.1 30.9 %all_to_all.10.x_ref = bf16[16,3,8,16,128]{4,3,2,1,0:T(8,128)(2,1)S(1)} all-to-all(bf16[16,3,8,16,128]{4,3,2,1,0:T(8,128)(2,1)S(1)} %to_channels.1), channel_id=1, replica_groups=mesh['ctx'=16,'tp'=8] {'ctx'}, dimensions={0} | all-to-all | bytes 3145728 | tf_op jit(solution)/shard_map/all_to_all | solution.py:198
  34.0 0.0 copy-done
  34.0 0.0 copy-done.1
  34.0 0.0 copy-done.2
  34.0 0.0 copy-done.3
  34.0 0.0 copy-done.4
  34.0 0.0 copy-done.5
  34.0 4.6 %convolve.1 = bf16[16,3,2,64,128]{4,3,2,1,0:T(8,128)(2,1)S(1)} custom-call(bf16[16,3,8,16,128]{4,3,2,1,0:T(8,128)(2,1)S(1)} %all_to_all.10.x_ref, f32[1,512]{1,0:T(1,128)S(1)} %bitcast.1, bf16[512,256]{1,0:T(8,128)(2,1)S(1)} %copy-done.2, bf16[256,512]{1,0:T(8,128)(2,1)S(1)} %copy-done.1, bf16[256,256]{1,0:T(8,128)(2,1)S(1)} %copy-done.4, ...), custom_call_target="tpu_custom_call" | custom-call | tf_op jit(solution)/shard_map/convolve/pallas_call | solution.py:201
  38.6 26.2 %all_to_all.11.in_ref = bf16[16,3,2,64,128]{4,3,2,1,0:T(8,128)(2,1)S(1)} all-to-all(bf16[16,3,2,64,128]{4,3,2,1,0:T(8,128)(2,1)S(1)} %convolve.1), channel_id=1, replica_groups=mesh['ctx'=16,'tp'=8] {'ctx'}, dimensions={0} | all-to-all | bytes 3145728 | tf_op jit(solution)/shard_map/all_to_all | solution.py:216
  64.8 1.5 %to_positions.1 = (bf16[512,512]{1,0:T(8,128)(2,1)}, bf16[512,512]{1,0:T(8,128)(2,1)}, bf16[512,512]{1,0:T(8,128)(2,1)}) custom-call(bf16[16,3,2,64,128]{4,3,2,1,0:T(8,128)(2,1)S(1)} %all_to_all.11.in_ref), custom_call_target="tpu_custom_call" | custom-call | tf_op jit(solution)/shard_map/to_positions/pallas_call | solution.py:217
Async XLA Ops:
  3.0 31.0 %copy-start = (f32[2,256,128]{2,1,0:T(8,128)S(1)}, f32[2,256,128]{2,1,0:T(8,128)}, u32[]{:S(2)}) copy-start(f32[2,256,128]{2,1,0:T(8,128)} %constant.14.clone.twist_ref) | copy-start | bytes 786436
  3.0 31.0 %copy-start.1 = (bf16[256,512]{1,0:T(8,128)(2,1)S(1)}, bf16[256,512]{1,0:T(8,128)(2,1)}, u32[]{:S(2)}) copy-start(bf16[256,512]{1,0:T(8,128)(2,1)} %constant.11.clone.back_ref) | copy-start | bytes 786436
  3.1 31.0 %copy-start.2 = (bf16[512,256]{1,0:T(8,128)(2,1)S(1)}, bf16[512,256]{1,0:T(8,128)(2,1)}, u32[]{:S(2)}) copy-start(bf16[512,256]{1,0:T(8,128)(2,1)} %constant.10.clone.wide_ref) | copy-start | bytes 786436
  3.1 31.0 %copy-start.3 = (bf16[256,256]{1,0:T(8,128)(2,1)S(1)}, bf16[256,256]{1,0:T(8,128)(2,1)}, u32[]{:S(2)}) copy-start(bf16[256,256]{1,0:T(8,128)(2,1)} %constant.13.clone.unlane_ref) | copy-start | bytes 393220
  3.1 31.0 %copy-start.4 = (bf16[256,256]{1,0:T(8,128)(2,1)S(1)}, bf16[256,256]{1,0:T(8,128)(2,1)}, u32[]{:S(2)}) copy-start(bf16[256,256]{1,0:T(8,128)(2,1)} %constant.12.clone.lane_ref) | copy-start | bytes 393220
  3.1 30.9 %copy-start.5 = (f32[512]{0:T(512)S(1)}, f32[512]{0:T(512)}, u32[]{:S(2)}) copy-start(f32[512]{0:T(512)} %param.11) | copy-start | bytes 6148
